TPU v7x, 512 devices: a whole 4x8x8 slice. The times are simulated.
512 devices in a mesh: tm: 32 (over y_lo, z), height: 16 (over x, y_hi, core).
Axes of the slice: x: 4, y: 8 (y_hi: 2, y_lo: 4; y = y_hi * 4 + y_lo), z: 8, core: 2. Of those that a mesh axis runs over, the one named last changes fastest.
Arguments:
- tokens: bfloat16 [256, 112, 7, 256], P('tm', 'height'), may hold values from -6 to 6
- norm_gain: float32 [256], replicated, may hold values from 0.1 to 1.9
- qkv_weight: bfloat16 [256, 768], replicated, may hold values from -0.75 to 0.75
- proj_weight: bfloat16 [256, 256], replicated, may hold values from -0.375 to 0.375
- rel_bias: float32 [8, 2535], replicated, may hold values from -4 to 320
- cotangent: bfloat16 [256, 112, 7, 256], P('tm', 'height'), may hold values from -6 to 6
Outputs:
- block_out: bfloat16 [256, 112, 7, 256], P('tm', 'height')
- token_grad: bfloat16 [256, 112, 7, 256], P('tm', 'height')
- proj_grad: float32 [256, 256], P(None, 'height')
All inputs are finite; a program needn't handle non-finite values.
Results may differ from a plain program's by a relative error of at most 0.0061.
Values may be sent and summed in bfloat16 or wider, within the bound.
A program may use at most 192 MiB of HBM per device.

v0:
```python
import jax
import jax.numpy as jnp
import numpy as np
from jax import lax
from jax.sharding import PartitionSpec as P

HEADS = 8


epsilon = 1e-05
masked_value = -1000000000.0


def passed_along(array, axis, by):
    length = lax.axis_size(axis)
    return lax.ppermute(array, axis, [(i, (i + by) % length) for i in range(length)])


def window_table(window_frames, window_rows):
    offset_span = 2 * window_rows - 1
    frame_ids = np.repeat(np.arange(window_frames), window_rows * window_rows)
    row_ids = np.tile(np.repeat(np.arange(window_rows), window_rows), window_frames)
    column_ids = np.tile(np.arange(window_rows), window_frames * window_rows)
    offsets = (
        (
            (frame_ids[:, None] - frame_ids[None, :] + window_frames - 1) * offset_span
            + row_ids[:, None]
            - row_ids[None, :]
            + window_rows
            - 1
        )
        * offset_span
        + column_ids[:, None]
        - column_ids[None, :]
        + window_rows
        - 1
    )
    return offsets.astype(np.int32)


def into_windows(grid, window_rows):
    window_frames, local_rows, full_width, channels = grid.shape
    blocks = full_width // window_rows
    pieces = grid.reshape(window_frames, local_rows, blocks, window_rows, channels)
    return pieces.transpose(2, 0, 1, 3, 4).reshape(
        blocks, window_frames * local_rows * window_rows, channels
    )


def from_windows(stacked, window_frames, window_rows):
    blocks, window_tokens, channels = stacked.shape
    pieces = stacked.reshape(blocks, window_frames, window_rows, window_rows, channels)
    return pieces.transpose(1, 2, 0, 3, 4).reshape(
        window_frames, window_rows, blocks * window_rows, channels
    )


def normalize(window_x, norm_gain):
    values = window_x.astype(jnp.float32)
    centred = values - jnp.mean(values, axis=-1, keepdims=True)
    inverse = lax.rsqrt(jnp.mean(centred * centred, axis=-1, keepdims=True) + epsilon)
    standard = centred * inverse
    return (values, standard, inverse, (standard * norm_gain).astype(jnp.bfloat16))


def attention_probs(queries, keys_all, bias_grid, same_region):
    scores = (
        jnp.einsum("qhd,khd->hqk", queries, keys_all, preferred_element_type=jnp.float32)
        + bias_grid
    )
    scores = jnp.where(same_region[None], scores, masked_value)
    raised = jnp.exp(scores - jnp.max(scores, axis=-1, keepdims=True))
    return raised / jnp.sum(raised, axis=-1, keepdims=True)


def forward_window(window_x, same_region, bias_grid, norm_gain, qkv_weight, proj_weight):
    window_tokens, channels = window_x.shape
    head_dim = channels // HEADS
    values, standard, inverse, normed = normalize(window_x, norm_gain)
    projected = jnp.dot(normed, qkv_weight, preferred_element_type=jnp.float32)
    queries = (
        (projected[:, :channels] * head_dim ** (-0.5))
        .astype(jnp.bfloat16)
        .reshape(window_tokens, HEADS, head_dim)
    )
    keys_all = (
        projected[:, channels : 2 * channels]
        .astype(jnp.bfloat16)
        .reshape(window_tokens, HEADS, head_dim)
    )
    values_all = (
        projected[:, 2 * channels :].astype(jnp.bfloat16).reshape(window_tokens, HEADS, head_dim)
    )
    softmaxed = attention_probs(queries, keys_all, bias_grid, same_region)
    soft_low = softmaxed.astype(jnp.bfloat16)
    attended = (
        jnp.einsum("hqk,khd->qhd", soft_low, values_all, preferred_element_type=jnp.float32)
        .reshape(window_tokens, channels)
        .astype(jnp.bfloat16)
    )
    output = (values + jnp.dot(attended, proj_weight, preferred_element_type=jnp.float32)).astype(
        jnp.bfloat16
    )
    return (output, queries, keys_all, values_all, attended, softmaxed)


def backward_window(
    window_x, grad_win, queries, keys_all, values_all, softmaxed, norm_gain, qkv_weight, proj_weight
):
    window_tokens, channels = window_x.shape
    head_dim = channels // HEADS
    values, standard, inverse, normed = normalize(window_x, norm_gain)
    soft_low = softmaxed.astype(jnp.bfloat16)
    grad_attended = (
        jnp.dot(grad_win, proj_weight.T, preferred_element_type=jnp.float32)
        .astype(jnp.bfloat16)
        .reshape(window_tokens, HEADS, head_dim)
    )
    grad_values = jnp.einsum(
        "hqk,qhd->khd", soft_low, grad_attended, preferred_element_type=jnp.float32
    ).astype(jnp.bfloat16)
    grad_probs = jnp.einsum(
        "qhd,khd->hqk", grad_attended, values_all, preferred_element_type=jnp.float32
    )
    grad_scores = (
        softmaxed * (grad_probs - jnp.sum(softmaxed * grad_probs, axis=-1, keepdims=True))
    ).astype(jnp.bfloat16)
    grad_queries = (
        jnp.einsum("hqk,khd->qhd", grad_scores, keys_all, preferred_element_type=jnp.float32)
        * head_dim ** (-0.5)
    ).astype(jnp.bfloat16)
    grad_keys = jnp.einsum(
        "hqk,qhd->khd", grad_scores, queries, preferred_element_type=jnp.float32
    ).astype(jnp.bfloat16)
    grad_joined = jnp.concatenate(
        [
            grad_queries.reshape(window_tokens, channels),
            grad_keys.reshape(window_tokens, channels),
            grad_values.reshape(window_tokens, channels),
        ],
        axis=1,
    )
    grad_normed = jnp.dot(grad_joined, qkv_weight.T, preferred_element_type=jnp.float32)
    scaled = grad_normed * norm_gain
    grad_branch = inverse * (
        scaled
        - jnp.mean(scaled, axis=-1, keepdims=True)
        - standard * jnp.mean(scaled * standard, axis=-1, keepdims=True)
    )
    return (grad_win.astype(jnp.float32) + grad_branch).astype(jnp.bfloat16)


def body(tokens, norm_gain, qkv_weight, proj_weight, rel_bias, cotangent):
    window_frames, window_rows, full_width, channels = tokens.shape
    frame_shift = window_frames // 2
    row_shift = window_rows // 2
    next_frames = passed_along(tokens[:frame_shift], "tm", -1)
    partial_tokens = jnp.concatenate([tokens[frame_shift:], next_frames], axis=0)
    next_rows = passed_along(partial_tokens[:, :row_shift], "height", -1)
    shifted_tokens = jnp.concatenate([partial_tokens[:, row_shift:], next_rows], axis=1)
    shifted_tokens = jnp.roll(shifted_tokens, -row_shift, axis=2)
    last_frame = lax.axis_index("tm") == lax.axis_size("tm") - 1
    last_row = lax.axis_index("height") == lax.axis_size("height") - 1
    frame_index = jnp.arange(window_frames)
    frame_region = jnp.where(
        last_frame, jnp.where(frame_index < window_frames - frame_shift, 1, 2), 0
    )
    row_index = jnp.arange(window_rows)
    row_region = jnp.where(last_row, jnp.where(row_index < window_rows - row_shift, 1, 2), 0)
    column_index = jnp.arange(full_width)
    column_region = jnp.where(
        column_index < full_width - window_rows,
        0,
        jnp.where(column_index < full_width - row_shift, 1, 2),
    )
    region = (
        frame_region[:, None, None] * 9
        + row_region[None, :, None] * 3
        + column_region[None, None, :]
    ).astype(jnp.int32)
    region_windows = into_windows(region[..., None], window_rows)[..., 0]
    same_all = region_windows[:, :, None] == region_windows[:, None, :]
    bias_grid = rel_bias[:, window_table(window_frames, window_rows)]
    token_windows = into_windows(shifted_tokens, window_rows)

    def forward_one(packed):
        return forward_window(packed[0], packed[1], bias_grid, norm_gain, qkv_weight, proj_weight)

    outputs, queries, keys_all, values_all, attended, softmaxed = lax.map(
        forward_one, (token_windows, same_all)
    )
    shifted_out = jnp.roll(from_windows(outputs, window_frames, window_rows), row_shift, axis=2)
    prior_rows = passed_along(shifted_out[:, window_rows - row_shift :], "height", 1)
    partial_out = jnp.concatenate([prior_rows, shifted_out[:, : window_rows - row_shift]], axis=1)
    prior_frames = passed_along(partial_out[window_frames - frame_shift :], "tm", 1)
    block_out = jnp.concatenate([prior_frames, partial_out[: window_frames - frame_shift]], axis=0)
    next_grad = passed_along(cotangent[:frame_shift], "tm", -1)
    partial_grad = jnp.concatenate([cotangent[frame_shift:], next_grad], axis=0)
    below_grad = passed_along(partial_grad[:, :row_shift], "height", -1)
    shifted_grad = jnp.concatenate([partial_grad[:, row_shift:], below_grad], axis=1)
    grad_windows = into_windows(jnp.roll(shifted_grad, -row_shift, axis=2), window_rows)

    def backward_one(packed):
        return backward_window(
            packed[0],
            packed[1],
            packed[2],
            packed[3],
            packed[4],
            packed[5],
            norm_gain,
            qkv_weight,
            proj_weight,
        )

    window_grads = lax.map(
        backward_one, (token_windows, grad_windows, queries, keys_all, values_all, softmaxed)
    )
    input_grads = jnp.roll(
        from_windows(window_grads, window_frames, window_rows), row_shift, axis=2
    )
    factor = float(
        window_frames * lax.axis_size("tm") * window_rows * lax.axis_size("height") * full_width
    ) ** (-0.5)
    partial_term = (
        lax.dot_general(
            attended.reshape(-1, channels),
            grad_windows.reshape(-1, channels),
            (((0,), (0,)), ((), ())),
            preferred_element_type=jnp.float32,
        )
        * factor
    )
    summed = lax.psum(partial_term, "tm")
    proj_grad = lax.psum_scatter(summed, "height", scatter_dimension=1, tiled=True)
    prior_grad_rows = passed_along(input_grads[:, window_rows - row_shift :], "height", 1)
    partial_back = jnp.concatenate(
        [prior_grad_rows, input_grads[:, : window_rows - row_shift]], axis=1
    )
    prior_grad_frames = passed_along(partial_back[window_frames - frame_shift :], "tm", 1)
    token_grad = jnp.concatenate(
        [prior_grad_frames, partial_back[: window_frames - frame_shift]], axis=0
    )
    return (block_out, token_grad, proj_grad)


def solution(mesh):
    placed = (P("tm", "height", None, None), P(), P(), P(), P(), P("tm", "height", None, None))
    return jax.shard_map(
        body,
        mesh=mesh,
        in_specs=placed,
        out_specs=(P("tm", "height", None, None), P("tm", "height", None, None), P(None, "height")),
        check_vma=False,
    )
```

profile of v0, /device:TPU:2, one launch (start us, length us, event | category | flops | bytes accessed | tf_op | source)
XLA Modules:
  0.0 651.5 jit_solution(4039819755497786183)
XLA Ops:
  7.2 1.1 fusion.42
  8.4 14.0 %collective-permute-start = (bf16[4,7,7,256]{3,0,2,1:T(4,128)(2,1)S(1)}, bf16[4,7,7,256]{3,0,2,1:T(4,128)(2,1)S(1)}, u32[]{:S(2)}, u32[]{:S(2)}) collective-permute-start(bf16[4,7,7,256]{3,0,2,1:T(4,128)(2,1)S(1)} %get-tuple-element.81), channel_id=1, source_target_pairs={{0,496},{16,0},{32,16},{48,32},{64,48},{80,64},{96,80},{112,96},{1... | collective-permute-start | bytes 301064 | tf_op jit(solution)/shard_map/ppermute | solution.py:16
  22.4 1.1 fusion.41
  23.5 2.5 collective-permute-start.4
  26.0 0.1 broadcast_add_fusion.1
  26.1 0.1 broadcast_add_fusion
  26.2 0.1 add.87
  26.3 1.2 pad_clamp_fusion
  27.5 0.9 broadcast_compare_fusion
  28.3 1.3 copy.52
  29.6 281.5 %gather_fusion = f32[153664,8]{1,0:T(8,128)} fusion(f32[8,2535]{0,1:T(8,128)S(1)} %copy.52, s32[154624]{0:T(1024)S(1)} %pad_clamp_fusion), kind=kCustom, calls=%fused_computation | custom fusion | bytes 10449152 | tf_op jit(solution)/shard_map/gather | solution.py:183
  311.1 52.6 %copy.54 = f32[392,392,8]{0,1,2:T(8,128)} copy(f32[392,392,8]{2,1,0:T(8,128)} %bitcast.3) | data formatting | bytes 9834496 | tf_op jit(solution)/shard_map/gather | solution.py:183
  363.8 3.9 collective-permute-start.1
  367.7 0.7 pad_maximum_fusion.8
  368.4 3.3 collective-permute-start.5
  371.8 0.1 fusion.32
  371.8 0.1 fusion.30
  371.9 0.1 fusion.36
  372.1 0.1 copy.47
  372.2 0.2 multiply_reduce_fusion.2
  372.4 0.1 copy.48
  372.6 0.1 rsqrt.15
  372.7 0.2 copy.46
  372.9 0.1 reshape.218
  373.0 0.1 div.35
  373.1 0.4 fusion.43
  373.6 0.1 copy.51
  373.8 0.1 copy.50
  373.9 4.1 fusion.1
  378.0 4.4 fusion.44
  382.4 0.2 copy-done.1
  382.6 0.9 copy.49
  383.5 0.1 squeeze.21
  383.6 0.9 convolution_convert_fusion.1
  384.6 1.9 copy.57
  386.5 4.2 multiply_reduce_fusion
  390.7 1.8 multiply_convert_fusion
  392.6 0.7 fusion.6
  393.3 1.0 convolution_convert_fusion
  394.3 6.1 fusion.10
  400.4 0.6 fusion.37
  401.1 0.3 add_convert_fusion
  401.4 0.1 reshape_transpose_reshape.9
  401.5 0.1 slice.134
  401.6 6.4 fusion.7
  408.0 1.0 convolution_multiply_fusion.2
  409.0 0.3 fusion.13
  409.2 0.1 reshape_transpose_reshape.8
  409.3 0.1 slice.126
  409.4 0.1 pad_maximum_fusion.6
  409.5 2.8 collective-permute-start.6
  412.4 0.1 pad_maximum_fusion.7
  412.4 3.9 collective-permute-start.2
  416.4 3.9 collective-permute-done.6
  420.2 0.1 fusion.20
  420.4 3.4 collective-permute-start.7
  423.8 0.1 fusion.21
  423.9 2.8 collective-permute-start.3
  426.7 4.6 collective-permute-done.7
  431.3 0.7 copy.62
  432.1 2.4 collective-permute-done.3
  434.5 0.7 copy.61
  435.2 58.3 %reduce-scatter.2.cloned.1.call-done = f32[256,16]{0,1:T(8,128)} async-done(((f32[256,256]{0,1:T(8,128)}), f32[256,16]{0,1:T(8,128)}) %reduce-scatter.2.cloned.1.call-update) | async-done | bytes 16400 | tf_op jit(solution)/shard_map/reduce_scatter | solution.py:235
  493.6 151.0 %psum.8 = f32[256,16]{0,1:T(8,128)} all-reduce(f32[256,16]{0,1:T(8,128)} %reduce-scatter.2.cloned.1.call-done), channel_id=1, replica_groups=mesh['tm'=32,'height'=16] {'tm'}, use_global_device_ids=true, to_apply=%region_7.8 | all-reduce | flops 4096 | bytes 32768 | tf_op jit(solution)/shard_map/psum | solution.py:234
  (49 shorter events, 0.6 us)
Async XLA Ops:
  7.2 365.9 %copy-start = (bf16[256,768]{1,0:T(8,128)(2,1)S(1)}, bf16[256,768]{1,0:T(8,128)(2,1)}, u32[]{:S(2)}) copy-start(bf16[256,768]{1,0:T(8,128)(2,1)} %param.10) | copy-start | bytes 1179652
  7.2 486.4 %reduce-scatter.2.cloned.1.call-start = ((), (), s32[]{:S(2)}) async-start(), calls=%async_computation.1 | async-start | bytes 278528 | tf_op jit(solution)/shard_map/reduce_scatter | solution.py:235
  8.4 355.4 %collective-permute-start = (bf16[4,7,7,256]{3,0,2,1:T(4,128)(2,1)S(1)}, bf16[4,7,7,256]{3,0,2,1:T(4,128)(2,1)S(1)}, u32[]{:S(2)}, u32[]{:S(2)}) collective-permute-start(bf16[4,7,7,256]{3,0,2,1:T(4,128)(2,1)S(1)} %get-tuple-element.81), channel_id=1, source_target_pairs={{0,496},{16,0},{32,16},{48,32},{64,48},{80,64},{96,80},{112,96},{1... | collective-permute-start | bytes 301064 | tf_op jit(solution)/shard_map/ppermute | solution.py:16
  23.5 344.3 %collective-permute-start.4 = (bf16[4,7,7,256]{3,0,2,1:T(4,128)(2,1)S(1)}, bf16[4,7,7,256]{3,0,2,1:T(4,128)(2,1)S(1)}, u32[]{:S(2)}, u32[]{:S(2)}) collective-permute-start(bf16[4,7,7,256]{3,0,2,1:T(4,128)(2,1)S(1)} %get-tuple-element.79), channel_id=1, source_target_pairs={{0,496},{16,0},{32,16},{48,32},{64,48},{80,64},{96,80},{112,96},{1... | collective-permute-start | bytes 301064 | tf_op jit(solution)/shard_map/ppermute | solution.py:16
  311.1 62.0 %copy-start.8 = (f32[256]{0:T(256)S(1)}, f32[256]{0:T(256)}, u32[]{:S(2)}) copy-start(f32[256]{0:T(256)} %param.9) | copy-start | bytes 3076
  363.8 8.1 %collective-permute-start.1 = (bf16[8,3,7,256]{3,0,2,1:T(8,128)(2,1)S(1)}, bf16[8,3,7,256]{3,0,2,1:T(8,128)(2,1)S(1)}, u32[]{:S(2)}, u32[]{:S(2)}) collective-permute-start(bf16[8,3,7,256]{3,0,2,1:T(8,128)(2,1)S(1)} %pad_maximum_fusion.9), channel_id=1, source_target_pairs={{0,15},{1,0},{2,1},{3,2},{4,3},{5,4},{6,5},{7,6},{8,7},{9,8},{10,9... | collective-permute-start | bytes 258056 | tf_op jit(solution)/shard_map/ppermute | solution.py:16
  368.4 15.0 %collective-permute-start.5 = (bf16[8,3,7,256]{3,0,2,1:T(8,128)(2,1)}, bf16[8,3,7,256]{3,0,2,1:T(8,128)(2,1)S(1)}, u32[]{:S(2)}, u32[]{:S(2)}) collective-permute-start(bf16[8,3,7,256]{3,0,2,1:T(8,128)(2,1)} %pad_maximum_fusion.8), channel_id=1, source_target_pairs={{0,15},{1,0},{2,1},{3,2},{4,3},{5,4},{6,5},{7,6},{8,7},{9,8},{10,9... | collective-permute-start | bytes 258056 | tf_op jit(solution)/shard_map/ppermute | solution.py:16
  373.9 4.1 copy-start.2
  378.0 4.6 copy-start.1
  378.0 5.6 copy-start.4
  384.6 6.1 slice-start
  386.5 4.2 slice-start.1
  390.7 2.5 copy-start.3
  392.6 1.7 copy-start.7
  394.3 7.3 %copy-start.6 = (bf16[392,256]{0,1:T(8,128)(2,1)S(1)}, bf16[392,256]{0,1:T(8,128)(2,1)}, u32[]{:S(2)}) copy-start(bf16[392,256]{0,1:T(8,128)(2,1)} %copy.49) | copy-start | bytes 602116
  401.6 7.4 %copy-start.5 = (bf16[256,256]{1,0:T(8,128)(2,1)S(1)}, bf16[256,256]{1,0:T(8,128)(2,1)}, u32[]{:S(2)}) copy-start(bf16[256,256]{1,0:T(8,128)(2,1)} %param.11) | copy-start | bytes 393220
  409.5 10.8 %collective-permute-start.6 = (bf16[8,3,7,256]{3,2,1,0:T(8,128)(2,1)S(1)}, bf16[8,3,7,256]{3,2,1,0:T(8,128)(2,1)S(1)}, u32[]{:S(2)}, u32[]{:S(2)}) collective-permute-start(bf16[8,3,7,256]{3,2,1,0:T(8,128)(2,1)S(1)} %pad_maximum_fusion.6), channel_id=1, source_target_pairs={{0,1},{1,2},{2,3},{3,4},{4,5},{5,6},{6,7},{7,8},{8,9},{9,10},{10,1... | collective-permute-start | bytes 258056 | tf_op jit(solution)/shard_map/ppermute | solution.py:16
  412.4 11.3 %collective-permute-start.2 = (bf16[8,3,7,256]{3,2,1,0:T(8,128)(2,1)S(1)}, bf16[8,3,7,256]{3,2,1,0:T(8,128)(2,1)S(1)}, u32[]{:S(2)}, u32[]{:S(2)}) collective-permute-start(bf16[8,3,7,256]{3,2,1,0:T(8,128)(2,1)S(1)} %pad_maximum_fusion.7), channel_id=1, source_target_pairs={{0,1},{1,2},{2,3},{3,4},{4,5},{5,6},{6,7},{7,8},{8,9},{9,10},{10,1... | collective-permute-start | bytes 258056 | tf_op jit(solution)/shard_map/ppermute | solution.py:16
  420.4 10.9 %collective-permute-start.7 = (bf16[4,7,7,256]{3,2,1,0:T(8,128)(2,1)S(1)}, bf16[4,7,7,256]{3,2,1,0:T(8,128)(2,1)S(1)}, u32[]{:S(2)}, u32[]{:S(2)}) collective-permute-start(bf16[4,7,7,256]{3,2,1,0:T(8,128)(2,1)S(1)} %get-tuple-element.74), channel_id=1, source_target_pairs={{0,16},{16,32},{32,48},{48,64},{64,80},{80,96},{96,112},{112,128},... | collective-permute-start | bytes 301064 | tf_op jit(solution)/shard_map/ppermute | solution.py:16
  423.9 10.6 %collective-permute-start.3 = (bf16[4,7,7,256]{3,2,1,0:T(8,128)(2,1)S(1)}, bf16[4,7,7,256]{3,2,1,0:T(8,128)(2,1)S(1)}, u32[]{:S(2)}, u32[]{:S(2)}) collective-permute-start(bf16[4,7,7,256]{3,2,1,0:T(8,128)(2,1)S(1)} %get-tuple-element.76), channel_id=1, source_target_pairs={{0,16},{16,32},{32,48},{48,64},{64,80},{80,96},{96,112},{112,128},... | collective-permute-start | bytes 301064 | tf_op jit(solution)/shard_map/ppermute | solution.py:16
Sparse Core Ops, SparseCore 0:
  412.5 81.0 reduce-scatter.1
where the time goes:
time: 653 us; the launch traced here: 651 us
  local copies, waits for them, and re-layouts  344 us (53%)
  blocking collectives  151 us (23%)
  waiting for transfers between devices  69.3 us (11%)
  starting transfers between devices  36.6 us (6%)
  matrix products  25.7 us (4%)
  between operations  14.6 us (2%)
  other arithmetic  10.4 us (2%)
    gather x2, local copies, waits for them, and re-layouts, body(): bias_grid = rel_bias[:, window_table(window_frames, window_rows)]  334 us
    psum x1, blocking collectives, body(): summed = lax.psum(partial_term, 'tm')  151 us
    reduce_scatter x1, waiting for transfers between devices, body(): lax.psum_scatter(summed, 'height', scatter_dimension=1, tiled=True)  58.3 us
    ppermute x8, starting transfers between devices, passed_along(): lax.ppermute(array, axis, [(i, (i + by) % length) for i in range(length)])  36.6 us
  transfers between devices with their start and end apart: 9, of which 4 were waited for; matrix products, arithmetic and copies ran while one was open for 54% of the time, Pallas kernels for 0%

commit v1 on v0

v1 whole, which is shorter than its diff:
```python
import functools

import jax
import jax.numpy as jnp
from jax import lax
from jax.experimental import pallas as pl
from jax.experimental.pallas import tpu as pltpu
from jax.sharding import PartitionSpec as P

HEADS = 8
DIM = 32
C = 256
FRAMES = 8
ROWS = 7
COLS = 7
PADDED = 8
GROUP = FRAMES * PADDED
N = ROWS * GROUP
FS = FRAMES // 2
RS = ROWS // 2
KEEP = ROWS - RS
OFFSETS = 2 * ROWS - 1
Z_SIZE = 8
MASKED = -1e9
EPSILON = 1e-5
F32 = jnp.float32
BF16 = jnp.bfloat16
MESH = pl.DeviceIdType.MESH


def dot(a, b, dims=((1,), (0,))):
    return lax.dot_general(a, b, (dims, ((), ())), preferred_element_type=F32)


def fold_max(x):
    return jnp.max(x.reshape(GROUP // 8, 8, N), axis=0)


def fold_sum(x):
    return jnp.sum(x.reshape(GROUP // 8, 8, N), axis=0)


def spread_bias(last_frame, rel, table, window, strip_even, strip_odd):
    table[...] = jnp.zeros_like(table)
    for d in range(OFFSETS):
        for t in range(2 * FRAMES - 1):
            start = (t * OFFSETS + d) * OFFSETS
            table[d, :, 16 * t : 16 * t + OFFSETS] = rel[:, start : start + OFFSETS]
    for d in range(OFFSETS):
        for t in range(FRAMES):
            start = (FRAMES - 1 - t) * 16
            window[d, t] = table[d, :, start : start + 128]
    lane = lax.broadcasted_iota(jnp.int32, (8, 128), 1)
    col_j = lax.broadcasted_iota(jnp.int32, (8, 128), 0)
    frame_i = (lane % GROUP) // PADDED
    col_i = lane % PADDED
    index = jnp.maximum(frame_i * 16 + col_i - col_j + COLS - 1, 0)
    same_cols = jnp.logical_and((col_j < RS) == (col_i < RS), col_j < COLS)
    low = lane < GROUP

    def one_head(h, carry):
        for t in range(FRAMES):
            same = jnp.logical_and(
                same_cols,
                jnp.logical_or(jnp.logical_not(last_frame), (frame_i < FS) == (t < FS)),
            )
            got = []
            for d in range(OFFSETS):
                source = jnp.broadcast_to(window[d, t, pl.ds(h, 1), :], (8, 128))
                value = jnp.take_along_axis(source, index, axis=1)
                got.append(jnp.where(same, value, MASKED))
            for p in range(7):
                pair = jnp.where(low, got[2 * p], got[min(2 * p + 1, OFFSETS - 1)])
                strip_even[h, 8 * t : 8 * t + 8, 128 * p : 128 * p + 128] = pair
            for p in range(6):
                pair = jnp.where(low, got[2 * p + 1], got[2 * p + 2])
                strip_odd[h, 8 * t : 8 * t + 8, 128 * p : 128 * p + 128] = pair
        return carry

    lax.fori_loop(0, HEADS, one_head, 0)


def body(
    n_tm, n_height, tok, gain, w_qkv, w_proj, rel, cot, out, grad, part,
    x_in, c_in, x_out, c_out, x_rows, c_rows, standard, inverse,
    table, window, strip_even, strip_odd, w_t, k_rows, v_rows, qkv_t, q_masked, g_masked,
    ga_t, scores, exp_f, exp_b, norm, att_t, grad_t, pg, recv_a, send_b, recv_b, send_c, recv_c,
    local_sem, in_send, in_recv, out_send, out_recv,
    a_send, a_recv, b_send, b_recv, c_send, c_recv,
):
    n_y = n_tm // Z_SIZE
    a, b = lax.axis_index("tm"), lax.axis_index("height")
    y, z = a // Z_SIZE, a % Z_SIZE
    a_prev, a_next = (a + n_tm - 1) % n_tm, (a + 1) % n_tm
    b_prev, b_next = (b + n_height - 1) % n_height, (b + 1) % n_height

    def place(tm, height):
        return {"tm": tm, "height": height}

    def remote(src, dst, send, recv, tm, height):
        return pltpu.make_async_remote_copy(
            src_ref=src, dst_ref=dst, send_sem=send, recv_sem=recv,
            device_id=place(tm, height), device_id_type=MESH,
        )

    barrier = pltpu.get_barrier_semaphore()
    partners = [(a_prev, b), (a, b_prev), (a_prev, b_prev), (a_next, b), (a, b_next), (a_next, b_next)]
    partners += [(a, (b + d) % n_height) for d in range(1, n_height)]
    partners += [(y * Z_SIZE + (z + d) % Z_SIZE, b) for d in range(1, Z_SIZE)]
    partners += [(((y + d) % n_y) * Z_SIZE + z, b) for d in range(1, n_y)]
    for tm, height in partners:
        pl.semaphore_signal(barrier, inc=1, device_id=place(tm, height), device_id_type=MESH)
    pl.semaphore_wait(barrier, len(partners))

    def halo_in(src, dst, which):
        return [
            remote(src.at[0:FS, RS:ROWS], dst.at[FS:FRAMES, 0:KEEP], in_send.at[which, 0], in_recv.at[which, 0], a_prev, b),
            remote(src.at[FS:FRAMES, 0:RS], dst.at[0:FS, KEEP:ROWS], in_send.at[which, 1], in_recv.at[which, 1], a, b_prev),
            remote(src.at[0:FS, 0:RS], dst.at[FS:FRAMES, KEEP:ROWS], in_send.at[which, 2], in_recv.at[which, 2], a_prev, b_prev),
        ]

    def halo_out(src, dst, which):
        return [
            remote(src.at[FS:FRAMES, 0:KEEP], dst.at[0:FS, RS:ROWS], out_send.at[which, 0], out_recv.at[which, 0], a_next, b),
            remote(src.at[0:FS, KEEP:ROWS], dst.at[FS:FRAMES, 0:RS], out_send.at[which, 1], out_recv.at[which, 1], a, b_next),
            remote(src.at[FS:FRAMES, KEEP:ROWS], dst.at[0:FS, 0:RS], out_send.at[which, 2], out_recv.at[which, 2], a_next, b_next),
        ]

    x_copies = halo_in(tok, x_in, 0)
    c_copies = halo_in(cot, c_in, 1)
    x_own = pltpu.make_async_copy(tok.at[FS:FRAMES, RS:ROWS], x_in.at[0:FS, 0:KEEP], local_sem.at[0])
    c_own = pltpu.make_async_copy(cot.at[FS:FRAMES, RS:ROWS], c_in.at[0:FS, 0:KEEP], local_sem.at[1])
    for copy in x_copies + [x_own] + c_copies + [c_own]:
        copy.start()

    spread_bias(a == n_tm - 1, rel, table, window, strip_even, strip_odd)
    w_t[...] = w_qkv[...].T
    q_masked[...] = jnp.zeros_like(q_masked)
    g_masked[...] = jnp.zeros_like(g_masked)
    x_rows[...] = jnp.zeros_like(x_rows)
    c_rows[...] = jnp.zeros_like(c_rows)
    row_i = lax.broadcasted_iota(jnp.int32, (1, N), 1) // GROUP
    last_row = b == n_height - 1
    cap_low = jnp.where(jnp.logical_and(last_row, row_i >= KEEP), MASKED, 3e38)
    cap_high = jnp.where(jnp.logical_and(last_row, row_i < KEEP), MASKED, 3e38)
    scale = DIM ** (-0.5)

    for copy in x_copies:
        copy.wait_recv()
    x_own.wait()
    for r in range(ROWS):
        x_rows[r, :, 0:COLS, :] = x_in[:, r].astype(F32)
    x = x_rows[...].reshape(N, C)
    centred = x - jnp.mean(x, axis=-1, keepdims=True)
    inv = lax.rsqrt(jnp.mean(centred * centred, axis=-1, keepdims=True) + EPSILON)
    std = centred * inv
    standard[...] = std
    inverse[...] = inv
    normed = (std * gain[...]).astype(BF16)
    k_rows[...] = dot(normed, w_qkv[:, C : 2 * C]).astype(BF16)
    v_rows[...] = dot(normed, w_qkv[:, 2 * C :]).astype(BF16)
    q_t = (dot(w_t[0:C], normed, ((1,), (1,))) * scale).astype(BF16)
    qkv_t[0:C] = q_t
    qkv_t[C:] = dot(w_t[C:], normed, ((1,), (1,))).astype(BF16)
    for h in range(HEADS):
        q_masked[h, DIM * h : DIM * h + DIM] = q_t[DIM * h : DIM * h + DIM]

    def forward_head(h, carry):
        top = pl.multiple_of(h * DIM, DIM)
        scores[...] = dot(k_rows[...], q_masked[h])
        peak = None
        for r in range(ROWS):
            start = (ROWS - 1 - r) * GROUP
            if r % 2 == 0:
                bias = strip_even[h, :, start : start + N]
            else:
                bias = strip_odd[h, :, start - GROUP : start - GROUP + N]
            s = scores[GROUP * r : GROUP * r + GROUP] + bias
            s = jnp.minimum(s, cap_low if r < KEEP else cap_high)
            scores[GROUP * r : GROUP * r + GROUP] = s
            most = fold_max(s)
            peak = most if peak is None else jnp.maximum(peak, most)
        peak = jnp.max(peak, axis=0, keepdims=True)
        total = None
        for r in range(ROWS):
            e = jnp.exp(scores[GROUP * r : GROUP * r + GROUP] - peak)
            exp_f[h, GROUP * r : GROUP * r + GROUP] = e
            exp_b[h, GROUP * r : GROUP * r + GROUP] = e.astype(BF16)
            more = fold_sum(e)
            total = more if total is None else total + more
        over = 1.0 / jnp.sum(total, axis=0, keepdims=True)
        norm[h] = over
        v_t = qkv_t[pl.ds(2 * C + top, DIM)]
        att_t[pl.ds(top, DIM)] = (dot(v_t, exp_b[h]) * over).astype(BF16)
        return carry

    lax.fori_loop(0, HEADS, forward_head, 0)

    att = att_t[...].T
    y_out = (x_rows[...].reshape(N, C) + dot(att, w_proj[...])).reshape(ROWS, FRAMES, PADDED, C)
    for r in range(ROWS):
        x_out[:, r] = y_out[r, :, 0:COLS, :].astype(BF16)
    sent = halo_out(x_out, out, 0)
    sent_own = pltpu.make_async_copy(x_out.at[0:FS, 0:KEEP], out.at[FS:FRAMES, RS:ROWS], local_sem.at[2])
    for copy in sent:
        copy.start()
    sent_own.start()

    for copy in c_copies:
        copy.wait_recv()
    c_own.wait()
    for r in range(ROWS):
        c_rows[r, :, 0:COLS, :] = c_in[:, r].astype(F32)
    cot_b = c_rows[...].reshape(N, C).astype(BF16)
    width = C // n_height
    pg[...] = dot(att_t[...], cot_b).T.reshape(n_height, width, C)
    a_copies = []
    for d in range(1, n_height):
        peer = (b + d) % n_height
        copy = remote(pg.at[peer], recv_a.at[d], a_send.at[d], a_recv.at[d], a, peer)
        copy.start()
        a_copies.append(copy)
    ga_t[...] = dot(w_proj[...], cot_b, ((1,), (1,)))

    def backward_head(h, carry):
        top = pl.multiple_of(h * DIM, DIM)
        over = norm[h]
        ga = (ga_t[pl.ds(top, DIM)] * over).astype(BF16)
        g_masked[h, pl.ds(top, DIM)] = ga
        grad_t[pl.ds(2 * C + top, DIM)] = dot(ga, exp_b[h], ((1,), (1,))).astype(BF16)
        scores[...] = dot(v_rows[...], g_masked[h])
        total = None
        for r in range(ROWS):
            more = fold_sum(scores[GROUP * r : GROUP * r + GROUP] * exp_f[h, GROUP * r : GROUP * r + GROUP])
            total = more if total is None else total + more
        mean = jnp.sum(total, axis=0, keepdims=True) * over
        for r in range(ROWS):
            rows = slice(GROUP * r, GROUP * r + GROUP)
            exp_b[h, rows] = (exp_f[h, rows] * (scores[rows] - mean)).astype(BF16)
        ds = exp_b[h]
        k_t = qkv_t[pl.ds(C + top, DIM)]
        q_t = qkv_t[pl.ds(top, DIM)]
        grad_t[pl.ds(top, DIM)] = (dot(k_t, ds) * scale).astype(BF16)
        grad_t[pl.ds(C + top, DIM)] = dot(q_t, ds, ((1,), (1,))).astype(BF16)
        return carry

    lax.fori_loop(0, 3, backward_head, 0)

    for copy in a_copies:
        copy.wait_recv()
    held = pg[b]
    for d in range(1, n_height):
        held = held + recv_a[d]
    send_b[...] = held
    recv_b[z] = held
    b_copies, b_waits = [], []
    for d in range(1, Z_SIZE):
        peer, source = (z + d) % Z_SIZE, (z + Z_SIZE - d) % Z_SIZE
        copy = remote(send_b, recv_b.at[z], b_send.at[d], b_recv.at[d], y * Z_SIZE + peer, b)
        copy.start()
        b_copies.append(copy)
        b_waits.append(remote(send_b, recv_b.at[source], b_send.at[d], b_recv.at[d], y * Z_SIZE + peer, b))

    lax.fori_loop(3, 6, backward_head, 0)

    for copy in b_waits:
        copy.wait_recv()
    held = recv_b[0]
    for i in range(1, Z_SIZE):
        held = held + recv_b[i]
    send_c[...] = held
    recv_c[y] = held
    c_stage, c_waits = [], []
    for d in range(1, n_y):
        peer, source = (y + d) % n_y, (y + n_y - d) % n_y
        copy = remote(send_c, recv_c.at[y], c_send.at[d], c_recv.at[d], peer * Z_SIZE + z, b)
        copy.start()
        c_stage.append(copy)
        c_waits.append(remote(send_c, recv_c.at[source], c_send.at[d], c_recv.at[d], peer * Z_SIZE + z, b))

    lax.fori_loop(6, HEADS, backward_head, 0)

    g = dot(w_qkv[...], grad_t[...]).T * gain[...]
    std = standard[...]
    branch = inverse[...] * (
        g - jnp.mean(g, axis=-1, keepdims=True) - std * jnp.mean(g * std, axis=-1, keepdims=True)
    )
    back = (c_rows[...].reshape(N, C) + branch).reshape(ROWS, FRAMES, PADDED, C)
    for r in range(ROWS):
        c_out[:, r] = back[r, :, 0:COLS, :].astype(BF16)
    returned = halo_out(c_out, grad, 1)
    returned_own = pltpu.make_async_copy(c_out.at[0:FS, 0:KEEP], grad.at[FS:FRAMES, RS:ROWS], local_sem.at[3])
    for copy in returned:
        copy.start()
    returned_own.start()

    for copy in c_waits:
        copy.wait_recv()
    held = recv_c[0]
    for i in range(1, n_y):
        held = held + recv_c[i]
    tokens = n_tm * FRAMES * n_height * ROWS * COLS
    part[...] = held * (float(tokens) ** (-0.5))

    for copy in sent + returned:
        copy.wait_recv()
    sent_own.wait()
    returned_own.wait()
    for copy in x_copies + c_copies + sent + returned + a_copies + b_copies + c_stage:
        copy.wait_send()


def solution(mesh):
    n_tm, n_height = mesh.shape["tm"], mesh.shape["height"]
    n_y = n_tm // Z_SIZE
    width = C // n_height
    local = (FRAMES, ROWS, COLS, C)
    anywhere = pl.BlockSpec(memory_space=pl.ANY)
    vmem = pl.BlockSpec(memory_space=pltpu.VMEM)
    dma = pltpu.SemaphoreType.DMA
    V = pltpu.VMEM
    call = pl.pallas_call(
        functools.partial(body, n_tm, n_height),
        out_shape=(
            jax.ShapeDtypeStruct(local, BF16),
            jax.ShapeDtypeStruct(local, BF16),
            jax.ShapeDtypeStruct((width, C), F32),
        ),
        in_specs=[anywhere, vmem, vmem, vmem, vmem, anywhere],
        out_specs=(anywhere, anywhere, vmem),
        scratch_shapes=[
            V(local, BF16), V(local, BF16), V(local, BF16), V(local, BF16),
            V((ROWS, FRAMES, PADDED, C), F32), V((ROWS, FRAMES, PADDED, C), F32),
            V((N, C), F32), V((N, 1), F32),
            V((OFFSETS, HEADS, 256), F32), V((OFFSETS, FRAMES, HEADS, 128), F32),
            V((HEADS, GROUP, 896), F32), V((HEADS, GROUP, 768), F32),
            V((3 * C, C), BF16), V((N, C), BF16), V((N, C), BF16), V((3 * C, N), BF16),
            V((HEADS, C, N), BF16), V((HEADS, C, N), BF16),
            V((C, N), F32), V((N, N), F32), V((HEADS, N, N), F32), V((HEADS, N, N), BF16),
            V((HEADS, 1, N), F32), V((C, N), BF16), V((3 * C, N), BF16),
            V((n_height, width, C), F32), V((n_height, width, C), F32),
            V((width, C), F32), V((Z_SIZE, width, C), F32),
            V((width, C), F32), V((n_y, width, C), F32),
            dma((4,)), dma((2, 3)), dma((2, 3)), dma((2, 3)), dma((2, 3)),
            dma((n_height,)), dma((n_height,)), dma((Z_SIZE,)), dma((Z_SIZE,)), dma((n_y,)), dma((n_y,)),
        ],
        compiler_params=pltpu.CompilerParams(
            collective_id=0, has_side_effects=True, vmem_limit_bytes=56 * 1024 * 1024
        ),
        cost_estimate=pl.CostEstimate(flops=1_000_000_000, bytes_accessed=3_000_000, transcendentals=1_600_000),
    )

    def device(tokens, norm_gain, qkv_weight, proj_weight, rel_bias, cotangent):
        block_out, token_grad, proj_grad = call(
            tokens, norm_gain.reshape(1, C), qkv_weight, proj_weight, rel_bias, cotangent
        )
        return block_out, token_grad, proj_grad.T

    whole = P("tm", "height", None, None)
    return jax.shard_map(
        device,
        mesh=mesh,
        in_specs=(whole, P(), P(), P(), P(), whole),
        out_specs=(whole, whole, P(None, "height")),
        check_vma=False,
    )
```

time: 653 us -> 64.7 us (0.10)
  the two profiles are of different devices: /device:TPU:2 before, /device:TPU:1 now
where the time goes in v1:
time: 64.7 us; the launch traced here: 63.8 us
  Pallas kernels  57.7 us (89%)
  local copies, waits for them, and re-layouts  5.46 us (8%)
  between operations  0.66 us (1%)
    pallas_call x1, Pallas kernels, device(): call(tokens, norm_gain.reshape(1, C), qkv_weight, proj_weight, rel_bias,...  57.7 us
    unnamed x11, local copies, waits for them, and re-layouts  5.46 us

profile of v1, /device:TPU:1, one launch (start us, length us, event | category | flops | bytes accessed | tf_op | source)
XLA Modules:
  0.0 63.8 jit_solution(9835459763399388287)
XLA Ops:
  0.6 0.0 copy-start.1
  0.6 1.7 %copy.9.tok = bf16[8,7,7,256]{3,2,1,0:T(8,128)(2,1)} copy(bf16[8,7,7,256]{3,0,2,1:T(8,128)(2,1)} %param.6) | data formatting | bytes 401408 | tf_op args[0]
  2.3 0.0 copy-done.1
  2.3 0.7 %copy.10.cot = bf16[8,7,7,256]{3,2,1,0:T(8,128)(2,1)} copy(bf16[8,7,7,256]{3,0,2,1:T(8,128)(2,1)S(1)} %copy-done.1) | data formatting | bytes 401408 | tf_op args[5]
  3.1 57.7 %shard_map.85 = (bf16[8,7,7,256]{3,2,1,0:T(8,128)(2,1)}, bf16[8,7,7,256]{3,2,1,0:T(8,128)(2,1)}, f32[16,256]{1,0:T(8,128)}) custom-call(bf16[8,7,7,256]{3,2,1,0:T(8,128)(2,1)} %copy.9.tok, f32[1,256]{1,0:T(1,128)} %bitcast.3, bf16[256,768]{1,0:T(8,128)(2,1)} %w_qkv.1, bf16[256,256]{1,0:T(8,128)(2,1)} %w_proj.1, f32[8,2535]{1,0:T(8,128)} %rel.1, ...), custom_call_target="tpu_custom_call" | custom-call | flops 1000000000 | bytes 3000000 | tf_op jit(solution)/shard_map/pallas_call | solution.py:354
  60.7 0.0 copy-start
  60.7 1.7 %copy.11 = bf16[8,7,7,256]{3,0,2,1:T(8,128)(2,1)} copy(bf16[8,7,7,256]{3,2,1,0:T(8,128)(2,1)} %get-tuple-element.9) | data formatting | bytes 401408
  62.4 0.0 copy-done
  62.4 0.0 copy-start.2
  62.5 0.7 %copy.12 = bf16[8,7,7,256]{3,0,2,1:T(8,128)(2,1)} copy(bf16[8,7,7,256]{3,2,1,0:T(8,128)(2,1)S(1)} %copy-done) | data formatting | bytes 401408
  63.2 0.0 copy-done.2
  63.2 0.6 copy.14
Async XLA Ops:
  0.6 1.7 %copy-start.1 = (bf16[8,7,7,256]{3,0,2,1:T(8,128)(2,1)S(1)}, bf16[8,7,7,256]{3,0,2,1:T(8,128)(2,1)}, u32[]{:S(2)}) copy-start(bf16[8,7,7,256]{3,0,2,1:T(8,128)(2,1)} %param.11) | copy-start | bytes 602116
  60.7 1.7 %copy-start = (bf16[8,7,7,256]{3,2,1,0:T(8,128)(2,1)S(1)}, bf16[8,7,7,256]{3,2,1,0:T(8,128)(2,1)}, u32[]{:S(2)}) copy-start(bf16[8,7,7,256]{3,2,1,0:T(8,128)(2,1)} %get-tuple-element.10) | copy-start | bytes 602116
  62.4 0.7 %copy-start.2 = (f32[16,256]{1,0:T(8,128)S(1)}, f32[16,256]{1,0:T(8,128)}, u32[]{:S(2)}) copy-start(f32[16,256]{1,0:T(8,128)} %get-tuple-element.8) | copy-start | bytes 49156

commit v2 on v1

v2 whole, which is shorter than its diff:
```python
import functools

import jax
import jax.numpy as jnp
from jax import lax
from jax.experimental import pallas as pl
from jax.experimental.pallas import tpu as pltpu
from jax.sharding import PartitionSpec as P

HEADS = 8
DIM = 32
C = 256
FRAMES = 8
ROWS = 7
COLS = 7
SLABS = ROWS * COLS
N = SLABS * FRAMES
BAND = COLS * FRAMES
FS = FRAMES // 2
RS = ROWS // 2
KEEP = ROWS - RS
MAIN = KEEP * COLS
TAIL = RS * COLS
HALF = MAIN // 2
PART = (TAIL + 1) // 2
OFFSETS = 2 * ROWS - 1
CHUNKS = ((0, 112), (112, 224), (224, 336), (336, N))
Z_SIZE = 8
MASKED = -1e9
EPSILON = 1e-5
F32 = jnp.float32
BF16 = jnp.bfloat16
MESH = pl.DeviceIdType.MESH


def dot(a, b, dims=((1,), (0,))):
    return lax.dot_general(a, b, (dims, ((), ())), preferred_element_type=F32)


def fold_max(x):
    return jnp.max(x.reshape(x.shape[0] // 8, 8, N), axis=0)


def fold_sum(x):
    return jnp.sum(x.reshape(x.shape[0] // 8, 8, N), axis=0)


def late(shape):
    return lax.broadcasted_iota(jnp.int32, shape, 1) >= FS


def swap(x):
    return pltpu.roll(x, FS, 1)


def pack(main, tail, to_side, to_above, to_corner):
    first, second = main[0:HALF], main[HALF:MAIN]
    to_side[...] = jnp.where(late(first.shape), swap(second), first).astype(BF16)
    first, second = tail[0:PART], tail[TAIL - PART : TAIL]
    to_above[...] = jnp.where(late(first.shape), first, swap(second)).astype(BF16)
    to_corner[...] = jnp.where(late(first.shape), swap(second), first).astype(BF16)


def unpack(own, side, above, corner):
    own, side = own.astype(F32), side[...].astype(F32)
    above, corner = above[...].astype(F32), corner[...].astype(F32)
    mask = late(side.shape)
    yield 0, jnp.where(mask, own[0:HALF], side)
    yield HALF, jnp.where(mask, own[HALF:MAIN], swap(side))
    mask = late(above.shape)
    yield MAIN, jnp.where(mask, above, corner)
    last = jnp.where(mask, swap(above), swap(corner))
    yield MAIN + PART, last[2 * PART - TAIL :]


def spread_bias(last_frame, last_row, rel, table, rows_ahead, rows_behind, strip, bias):
    table[...] = jnp.zeros_like(table)
    for d in range(OFFSETS):
        for t in range(2 * FRAMES - 1):
            start = (t * OFFSETS + d) * OFFSETS
            table[d, :, 16 * t + 16 : 16 * t + 16 + OFFSETS] = rel[:, start : start + OFFSETS]
    lane = lax.broadcasted_iota(jnp.int32, (8, 128), 1)
    for tile in range(rows_ahead.shape[1]):
        place = (lane + 128 * tile) % BAND
        spot = (lane % FRAMES) * 16 + place // FRAMES
        first, last = 128 * tile // BAND, min((128 * tile + 127) // BAND, OFFSETS - 1)
        for c in range(COLS):
            same = (place < RS * FRAMES) == (c < RS)
            for side, rows in ((0, rows_behind), (128, rows_ahead)):
                value = None
                for d in range(first, last + 1):
                    piece = jnp.take_along_axis(table[d, :, side : side + 128], spot + (COLS - 1 - c), axis=1)
                    value = piece if value is None else jnp.where(lane >= BAND * d - 128 * tile, piece, value)
                rows[c, tile] = jnp.where(same, value, MASKED)
    frame_j = (lax.broadcasted_iota(jnp.int32, (8, 128), 0) + FS) % FRAMES
    frame_i = (lane + FS) % FRAMES
    index = (lane // FRAMES) * FRAMES + (frame_i - frame_j + FRAMES) % FRAMES
    forward = frame_i >= frame_j
    same_frames = jnp.logical_or(jnp.logical_not(last_frame), (frame_i < FS) == (frame_j < FS))
    row_i = lax.broadcasted_iota(jnp.int32, (1, N), 1) // BAND
    cap_low = jnp.where(jnp.logical_and(last_row, row_i >= KEEP), MASKED, 3e38)
    cap_high = jnp.where(jnp.logical_and(last_row, row_i < KEEP), MASKED, 3e38)

    def one_head(h, carry):
        for columns in ((0, 1, 2), (3, 4), (5, 6)):
            found = []
            for c in columns:
                for tile in range(strip.shape[1] // 128):
                    one = jnp.broadcast_to(rows_ahead[c, tile, pl.ds(h, 1), :], (8, 128))
                    two = jnp.broadcast_to(rows_behind[c, tile, pl.ds(h, 1), :], (8, 128))
                    one = jnp.take_along_axis(one, index, axis=1)
                    two = jnp.take_along_axis(two, index, axis=1)
                    found.append(jnp.where(same_frames, jnp.where(forward, one, two), MASKED))
            for n, value in enumerate(found):
                c, tile = columns[n // 6], n % 6
                strip[8 * c : 8 * c + 8, 128 * tile : 128 * tile + 128] = value
        for rows in ((0, 1, 2, 3), (4, 5, 6)):
            found = []
            for r in rows:
                start = (ROWS - 1 - r) * BAND
                found.append(jnp.minimum(strip[:, start : start + N], cap_low if r < KEEP else cap_high))
            for r, value in zip(rows, found):
                bias[h, BAND * r : BAND * r + BAND] = value
        return carry

    lax.fori_loop(0, HEADS, one_head, 0)


def body(
    n_tm, n_height, tok, gain, w_qkv, w_proj, rel, cot, out, grad, part,
    x_sent, c_sent, x_got, c_got, y_sent, g_sent, y_got, g_got, y_own, g_own, order, x_rows, c_rows, standard, inverse,
    table, rows_ahead, rows_behind, strip, bias, w_t, k_rows, v_rows, qkv_t, q_masked, g_masked,
    ga_t, scores, exp_f, exp_b, norm, att_t, grad_t, pg, got_core, held_core, got_z, held_z, got_xy, got_tm,
    in_send, in_recv, out_send, out_recv, core_send, core_recv,
    z_send, z_recv, xy_send, xy_recv, tm_send, tm_recv,
):
    n_xy = n_height // 2
    a, b = lax.axis_index("tm"), lax.axis_index("height")
    y, z = a // Z_SIZE, a % Z_SIZE
    xy, core = b // 2, b % 2
    a_prev, a_next = (a + n_tm - 1) % n_tm, (a + 1) % n_tm
    b_prev, b_next = (b + n_height - 1) % n_height, (b + 1) % n_height

    def place(tm, height):
        return {"tm": tm, "height": height}

    def remote(src, dst, send, recv, tm, height):
        return pltpu.make_async_remote_copy(
            src_ref=src, dst_ref=dst, send_sem=send, recv_sem=recv,
            device_id=place(tm, height), device_id_type=MESH,
        )

    barrier = pltpu.get_barrier_semaphore()
    stretch = pl.when(a < n_tm)
    partners = [(a_prev, b), (a, b_prev), (a_prev, b_prev), (a_next, b), (a, b_next), (a_next, b_next)]
    partners += [(a, xy * 2 + 1 - core)]
    partners += [(a, (xy + d) % n_xy * 2 + core) for d in range(1, n_xy)]
    partners += [((a + d) % n_tm, b) for d in range(1, n_tm)]
    for tm, height in partners:
        pl.semaphore_signal(barrier, inc=1, device_id=place(tm, height), device_id_type=MESH)
    pack(tok[TAIL:].astype(F32), tok[0:TAIL].astype(F32), *x_sent)
    pl.semaphore_wait(barrier, len(partners))

    def halo(src, dst, send, recv, tm, height):
        return [
            remote(src[0], dst[0], send.at[0], recv.at[0], tm, b),
            remote(src[1], dst[1], send.at[1], recv.at[1], a, height),
            remote(src[2], dst[2], send.at[2], recv.at[2], tm, height),
        ]

    x_copies = halo(x_sent, x_got, in_send.at[0], in_recv.at[0], a_prev, b_prev)
    c_copies = halo(c_sent, c_got, in_send.at[1], in_recv.at[1], a_prev, b_prev)
    for copy in x_copies:
        copy.start()

    scale = DIM ** (-0.5)

    @stretch
    def alone():
        pack(cot[TAIL:].astype(F32), cot[0:TAIL].astype(F32), *c_sent)
        spread_bias(
            a == n_tm - 1, b == n_height - 1, rel, table, rows_ahead, rows_behind, strip, bias
        )
        w_t[...] = w_qkv[...].T
        q_masked[...] = jnp.zeros_like(q_masked)
        g_masked[...] = jnp.zeros_like(g_masked)
        column = lax.broadcasted_iota(jnp.int32, (C, C), 1)
        e, q = column % 2, column // 2 % n_xy
        z_of, core_of = column // (2 * n_xy) % Z_SIZE, column // (2 * n_xy * Z_SIZE)
        channel = (q * 2 + core_of) * (2 * Z_SIZE) + z_of * 2 + e
        order[...] = (lax.broadcasted_iota(jnp.int32, (C, C), 0) == channel).astype(BF16)

    for copy in x_copies:
        copy.wait_recv()
    for copy in c_copies:
        copy.start()
    @stretch
    def forward():
        for at, value in unpack(tok[TAIL:], *x_got):
            x_rows[at : at + value.shape[0]] = value
        x = x_rows[...].reshape(N, C)
        centred = x - jnp.mean(x, axis=-1, keepdims=True)
        inv = lax.rsqrt(jnp.mean(centred * centred, axis=-1, keepdims=True) + EPSILON)
        std = centred * inv
        standard[...] = std
        inverse[...] = inv
        normed = (std * gain[...]).astype(BF16)
        k_rows[...] = dot(normed, w_qkv[:, C : 2 * C]).astype(BF16)
        v_rows[...] = dot(normed, w_qkv[:, 2 * C :]).astype(BF16)
        q_t = (dot(w_t[0:C], normed, ((1,), (1,))) * scale).astype(BF16)
        qkv_t[0:C] = q_t
        qkv_t[C:] = dot(w_t[C:], normed, ((1,), (1,))).astype(BF16)
        for h in range(HEADS):
            q_masked[h, DIM * h : DIM * h + DIM] = q_t[DIM * h : DIM * h + DIM]

        def forward_head(h, carry):
            top = pl.multiple_of(h * DIM, DIM)
            scores[...] = dot(k_rows[...], q_masked[h])
            peak = None
            for lo, hi in CHUNKS:
                s = scores[lo:hi] + bias[h, lo:hi]
                scores[lo:hi] = s
                most = fold_max(s)
                peak = most if peak is None else jnp.maximum(peak, most)
            peak = jnp.max(peak, axis=0, keepdims=True)
            total = None
            for lo, hi in CHUNKS:
                e = jnp.exp(scores[lo:hi] - peak)
                exp_f[h, lo:hi] = e
                exp_b[h, lo:hi] = e.astype(BF16)
                more = fold_sum(e)
                total = more if total is None else total + more
            over = 1.0 / jnp.sum(total, axis=0, keepdims=True)
            norm[h] = over
            v_t = qkv_t[pl.ds(2 * C + top, DIM)]
            att_t[pl.ds(top, DIM)] = (dot(v_t, exp_b[h]) * over).astype(BF16)
            return carry

        lax.fori_loop(0, HEADS, forward_head, 0)

        att = att_t[...].T
        y_out = (x_rows[...].reshape(N, C) + dot(att, w_proj[...])).reshape(SLABS, FRAMES, C)
        pack(y_out[0:MAIN], y_out[MAIN:], *y_sent)
        y_own[...] = y_out[0:MAIN].astype(BF16)

    sent = halo(y_sent, y_got, out_send.at[0], out_recv.at[0], a_next, b_next)
    for copy in sent:
        copy.start()

    for copy in c_copies:
        copy.wait_recv()
    @stretch
    def partial_gradient():
        for at, value in unpack(cot[TAIL:], *c_got):
            c_rows[at : at + value.shape[0]] = value
        cot_b = c_rows[...].reshape(N, C).astype(BF16)
        cot_order = dot(cot_b, order[...]).astype(BF16)
        pg[...] = dot(att_t[...], cot_order).T.reshape(2, Z_SIZE, 2 * n_xy, C)

    to_core = remote(pg.at[1 - core], got_core, core_send.at[0], core_recv.at[0], a, xy * 2 + 1 - core)
    to_core.start()

    def backward_head(h, carry):
        top = pl.multiple_of(h * DIM, DIM)
        over = norm[h]
        ga = (ga_t[pl.ds(top, DIM)] * over).astype(BF16)
        g_masked[h, pl.ds(top, DIM)] = ga
        grad_t[pl.ds(2 * C + top, DIM)] = dot(ga, exp_b[h], ((1,), (1,))).astype(BF16)
        scores[...] = dot(v_rows[...], g_masked[h])
        total = None
        for lo, hi in CHUNKS:
            more = fold_sum(scores[lo:hi] * exp_f[h, lo:hi])
            total = more if total is None else total + more
        mean = jnp.sum(total, axis=0, keepdims=True) * over
        for lo, hi in CHUNKS:
            exp_b[h, lo:hi] = (exp_f[h, lo:hi] * (scores[lo:hi] - mean)).astype(BF16)
        ds = exp_b[h]
        k_t = qkv_t[pl.ds(C + top, DIM)]
        q_t = qkv_t[pl.ds(top, DIM)]
        grad_t[pl.ds(top, DIM)] = (dot(k_t, ds) * scale).astype(BF16)
        grad_t[pl.ds(C + top, DIM)] = dot(q_t, ds, ((1,), (1,))).astype(BF16)
        return carry

    @stretch
    def backward_first():
        cot_b = c_rows[...].reshape(N, C).astype(BF16)
        ga_t[...] = dot(w_proj[...], cot_b, ((1,), (1,)))
        lax.fori_loop(0, 2, backward_head, 0)

    to_core.wait_recv()
    held_core[...] = pg[core] + got_core[...]
    z_copies = []
    for d in range(1, Z_SIZE):
        peer = (z + d) % Z_SIZE
        copy = remote(held_core.at[peer], got_z.at[d], z_send.at[d], z_recv.at[d], y * Z_SIZE + peer, b)
        copy.start()
        z_copies.append(copy)

    @stretch
    def backward_second():
        lax.fori_loop(2, 5, backward_head, 0)

    for copy in z_copies:
        copy.wait_recv()
    held = held_core[z]
    for d in range(1, Z_SIZE):
        held = held + got_z[d]
    for i in range(n_xy):
        held_z[i, 0:2] = held[2 * i : 2 * i + 2, 0:128]
        held_z[i, 2:4] = held[2 * i : 2 * i + 2, 128:256]
    xy_copies = []
    for d in range(1, n_xy):
        peer = (xy + d) % n_xy
        copy = remote(held_z.at[peer], got_xy.at[d], xy_send.at[d], xy_recv.at[d], a, peer * 2 + core)
        copy.start()
        xy_copies.append(copy)

    @stretch
    def backward_third():
        lax.fori_loop(5, HEADS, backward_head, 0)

    for copy in xy_copies:
        copy.wait_recv()
    held = held_z[xy]
    for d in range(1, n_xy):
        held = held + got_xy[d]
    got_tm[a] = held
    tm_copies, tm_waits = [], []
    for d in range(1, n_tm):
        peer, source = (a + d) % n_tm, (a + n_tm - d) % n_tm
        copy = remote(got_tm.at[a], got_tm.at[a], tm_send.at[d], tm_recv.at[d], peer, b)
        copy.start()
        tm_copies.append(copy)
        tm_waits.append(remote(got_tm.at[a], got_tm.at[source], tm_send.at[d], tm_recv.at[d], peer, b))

    @stretch
    def backward_rest():
        g = dot(w_qkv[...], grad_t[...]).T * gain[...]
        std = standard[...]
        branch = inverse[...] * (
            g - jnp.mean(g, axis=-1, keepdims=True) - std * jnp.mean(g * std, axis=-1, keepdims=True)
        )
        back = (c_rows[...].reshape(N, C) + branch).reshape(SLABS, FRAMES, C)
        pack(back[0:MAIN], back[MAIN:], *g_sent)
        g_own[...] = back[0:MAIN].astype(BF16)

    returned = halo(g_sent, g_got, out_send.at[1], out_recv.at[1], a_next, b_next)
    for copy in returned:
        copy.start()

    def finish(result, own, got):
        for at, value in unpack(own, *got):
            at = (at + TAIL) % SLABS
            result[at : at + value.shape[0]] = value.astype(BF16)

    for copy in sent:
        copy.wait_recv()
    finish(out, y_own[...], y_got)
    for copy in tm_waits:
        copy.wait_recv()
    tokens = n_tm * FRAMES * n_height * ROWS * COLS
    for i in range(Z_SIZE):
        held = got_tm[i]
        for j in range(1, n_tm // Z_SIZE):
            held = held + got_tm[j * Z_SIZE + i]
        held = held * (float(tokens) ** (-0.5))
        part[2 * i : 2 * i + 2, 0:128] = held[0:2]
        part[2 * i : 2 * i + 2, 128:256] = held[2:4]

    for copy in returned:
        copy.wait_recv()
    finish(grad, g_own[...], g_got)
    for copy in x_copies + c_copies + sent + returned + [to_core] + z_copies + xy_copies + tm_copies:
        copy.wait_send()


def solution(mesh):
    n_tm, n_height = mesh.shape["tm"], mesh.shape["height"]
    n_xy = n_height // 2
    width = C // n_height
    local = (SLABS, FRAMES, C)
    vmem = pl.BlockSpec(memory_space=pltpu.VMEM)
    dma = pltpu.SemaphoreType.DMA
    V = pltpu.VMEM
    call = pl.pallas_call(
        functools.partial(body, n_tm, n_height),
        out_shape=(
            jax.ShapeDtypeStruct(local, BF16),
            jax.ShapeDtypeStruct(local, BF16),
            jax.ShapeDtypeStruct((width, C), F32),
        ),
        in_specs=[vmem] * 6,
        out_specs=(vmem, vmem, vmem),
        scratch_shapes=[
            *[[V((n, FRAMES, C), BF16) for n in (HALF, PART, PART)] for _ in range(8)],
            V((MAIN, FRAMES, C), BF16), V((MAIN, FRAMES, C), BF16), V((C, C), BF16), V(local, F32), V(local, F32), V((N, C), F32), V((N, 1), F32),
            V((OFFSETS, HEADS, 256), F32),
            V((COLS, 6, HEADS, 128), F32), V((COLS, 6, HEADS, 128), F32), V((BAND, 768), F32), V((HEADS, N, N), F32),
            V((3 * C, C), BF16), V((N, C), BF16), V((N, C), BF16), V((3 * C, N), BF16),
            V((HEADS, C, N), BF16), V((HEADS, C, N), BF16),
            V((C, N), F32), V((N, N), F32), V((HEADS, N, N), F32), V((HEADS, N, N), BF16),
            V((HEADS, 1, N), F32), V((C, N), BF16), V((3 * C, N), BF16),
            V((2, Z_SIZE, 2 * n_xy, C), F32), V((Z_SIZE, 2 * n_xy, C), F32), V((Z_SIZE, 2 * n_xy, C), F32),
            V((Z_SIZE, 2 * n_xy, C), F32), V((n_xy, 4, 128), F32), V((n_xy, 4, 128), F32), V((n_tm, 4, 128), F32),
            dma((2, 3)), dma((2, 3)), dma((2, 3)), dma((2, 3)),
            dma((1,)), dma((1,)), dma((Z_SIZE,)), dma((Z_SIZE,)),
            dma((n_xy,)), dma((n_xy,)), dma((n_tm,)), dma((n_tm,)),
        ],
        compiler_params=pltpu.CompilerParams(
            collective_id=0, has_side_effects=True, vmem_limit_bytes=56 * 1024 * 1024
        ),
        cost_estimate=pl.CostEstimate(flops=1_000_000_000, bytes_accessed=3_000_000, transcendentals=1_600_000),
    )

    def device(tokens, norm_gain, qkv_weight, proj_weight, rel_bias, cotangent):
        def inside(grid):
            return grid.transpose(1, 2, 0, 3).reshape(local)

        def outside(slabs):
            return slabs.reshape(ROWS, COLS, FRAMES, C).transpose(2, 0, 1, 3)

        block_out, token_grad, proj_grad = call(
            inside(tokens), norm_gain.reshape(1, C), qkv_weight, proj_weight, rel_bias, inside(cotangent)
        )
        return outside(block_out), outside(token_grad), proj_grad.T

    whole = P("tm", "height", None, None)
    return jax.shard_map(
        device,
        mesh=mesh,
        in_specs=(whole, P(), P(), P(), P(), whole),
        out_specs=(whole, whole, P(None, "height")),
        check_vma=False,
    )
```

time: 64.7 us -> 56.6 us (0.87); the launches traced: 63.8 us -> 56.4 us
  Pallas kernels: 57.7 us -> 52.8 us
  local copies, waits for them, and re-layouts: 5.46 us -> 2.99 us
    pallas_call x1, Pallas kernels: 57.7 us -> 52.8 us  [device(): call(inside(tokens), norm_gain.reshape(1, C), qkv_weight, proj_weight, re...]
    unnamed x11 -> x7, local copies, waits for them, and re-layouts: 5.46 us -> 2.99 us
where the time goes in v2:
time: 56.6 us; the launch traced here: 56.4 us
  Pallas kernels  52.8 us (93%)
  local copies, waits for them, and re-layouts  2.99 us (5%)
  between operations  0.65 us (1%)
    pallas_call x1, Pallas kernels, device(): call(inside(tokens), norm_gain.reshape(1, C), qkv_weight, proj_weight, re...  52.8 us
    unnamed x7, local copies, waits for them, and re-layouts  2.99 us

profile of v2, /device:TPU:1, one launch (start us, length us, event | category | flops | bytes accessed | tf_op | source)
XLA Modules:
  0.0 56.4 jit_solution(8727855041825028859)
XLA Ops:
  0.6 52.8 %shard_map.85 = (bf16[49,8,256]{2,1,0:T(8,128)(2,1)}, bf16[49,8,256]{2,1,0:T(8,128)(2,1)}, f32[16,256]{1,0:T(8,128)}) custom-call(bf16[49,8,256]{2,1,0:T(8,128)(2,1)} %bitcast.17, f32[1,256]{1,0:T(1,128)} %bitcast.19, bf16[256,768]{1,0:T(8,128)(2,1)} %w_qkv.1, bf16[256,256]{1,0:T(8,128)(2,1)} %w_proj.1, f32[8,2535]{1,0:T(8,128)} %rel.1, ...), custom_call_target="tpu_custom_call" | custom-call | flops 1000000000 | bytes 3000000 | tf_op jit(solution)/shard_map/pallas_call | solution.py:422
  53.4 0.0 copy-start
  53.4 1.7 %copy.12 = bf16[8,7,7,256]{3,0,2,1:T(8,128)(2,1)} copy(bf16[8,7,7,256]{3,0,2,1:T(8,128)(2,1)} %bitcast.15) | data formatting | bytes 401408
  55.1 0.0 copy-done
  55.1 0.0 copy-start.1
  55.1 0.7 %copy.13 = bf16[8,7,7,256]{3,0,2,1:T(8,128)(2,1)} copy(bf16[8,7,7,256]{3,0,2,1:T(8,128)(2,1)S(1)} %bitcast.14) | data formatting | bytes 401408
  55.8 0.0 copy-done.1
  55.8 0.6 %copy.14 = f32[256,16]{0,1:T(8,128)} copy(f32[256,16]{0,1:T(8,128)S(1)} %bitcast.16) | data formatting | bytes 32768
Async XLA Ops:
  53.4 1.7 %copy-start = (bf16[49,8,256]{2,1,0:T(8,128)(2,1)S(1)}, bf16[49,8,256]{2,1,0:T(8,128)(2,1)}, u32[]{:S(2)}) copy-start(bf16[49,8,256]{2,1,0:T(8,128)(2,1)} %get-tuple-element.7) | copy-start | bytes 602116
  55.1 0.7 %copy-start.1 = (f32[16,256]{1,0:T(8,128)S(1)}, f32[16,256]{1,0:T(8,128)}, u32[]{:S(2)}) copy-start(f32[16,256]{1,0:T(8,128)} %get-tuple-element.8) | copy-start | bytes 49156

commit v3 on v2

--- a/solution.py
+++ b/solution.py
@@ -236,7 +236,10 @@
             att_t[pl.ds(top, DIM)] = (dot(v_t, exp_b[h]) * over).astype(BF16)
             return carry
 
-        lax.fori_loop(0, HEADS, forward_head, 0)
+        def forward_pair(i, carry):
+            return forward_head(2 * i + 1, forward_head(2 * i, carry))
+
+        lax.fori_loop(0, HEADS // 2, forward_pair, 0)
 
         att = att_t[...].T
         y_out = (x_rows[...].reshape(N, C) + dot(att, w_proj[...])).reshape(SLABS, FRAMES, C)
@@ -319,20 +322,6 @@
     def backward_third():
         lax.fori_loop(5, HEADS, backward_head, 0)
 
-    for copy in xy_copies:
-        copy.wait_recv()
-    held = held_z[xy]
-    for d in range(1, n_xy):
-        held = held + got_xy[d]
-    got_tm[a] = held
-    tm_copies, tm_waits = [], []
-    for d in range(1, n_tm):
-        peer, source = (a + d) % n_tm, (a + n_tm - d) % n_tm
-        copy = remote(got_tm.at[a], got_tm.at[a], tm_send.at[d], tm_recv.at[d], peer, b)
-        copy.start()
-        tm_copies.append(copy)
-        tm_waits.append(remote(got_tm.at[a], got_tm.at[source], tm_send.at[d], tm_recv.at[d], peer, b))
-
     @stretch
     def backward_rest():
         g = dot(w_qkv[...], grad_t[...]).T * gain[...]
@@ -347,6 +336,20 @@
     returned = halo(g_sent, g_got, out_send.at[1], out_recv.at[1], a_next, b_next)
     for copy in returned:
         copy.start()
+
+    for copy in xy_copies:
+        copy.wait_recv()
+    held = held_z[xy]
+    for d in range(1, n_xy):
+        held = held + got_xy[d]
+    got_tm[a] = held
+    tm_copies, tm_waits = [], []
+    for d in range(1, n_tm):
+        peer, source = (a + d) % n_tm, (a + n_tm - d) % n_tm
+        copy = remote(got_tm.at[a], got_tm.at[a], tm_send.at[d], tm_recv.at[d], peer, b)
+        copy.start()
+        tm_copies.append(copy)
+        tm_waits.append(remote(got_tm.at[a], got_tm.at[source], tm_send.at[d], tm_recv.at[d], peer, b))
 
     def finish(result, own, got):
         for at, value in unpack(own, *got):

time: 56.6 us -> 54.3 us (0.959)
  Pallas kernels: 52.8 us -> 50.4 us
    pallas_call x1, Pallas kernels: 52.8 us -> 50.4 us  [device(): call(inside(tokens), norm_gain.reshape(1, C), qkv_weight, proj_weight, re...]
where the time goes in v3:
time: 54.3 us; the launch traced here: 54.1 us
  Pallas kernels  50.4 us (93%)
  local copies, waits for them, and re-layouts  2.99 us (6%)
  between operations  0.65 us (1%)
    pallas_call x1, Pallas kernels, device(): call(inside(tokens), norm_gain.reshape(1, C), qkv_weight, proj_weight, re...  50.4 us
    unnamed x7, local copies, waits for them, and re-layouts  2.99 us

profile of v3, /device:TPU:1, one launch (start us, length us, event | category | flops | bytes accessed | tf_op | source)
XLA Modules:
  0.0 54.1 jit_solution(9107243273437360388)
XLA Ops:
  0.6 50.4 %shard_map.85 = (bf16[49,8,256]{2,1,0:T(8,128)(2,1)}, bf16[49,8,256]{2,1,0:T(8,128)(2,1)}, f32[16,256]{1,0:T(8,128)}) custom-call(bf16[49,8,256]{2,1,0:T(8,128)(2,1)} %bitcast.17, f32[1,256]{1,0:T(1,128)} %bitcast.19, bf16[256,768]{1,0:T(8,128)(2,1)} %w_qkv.1, bf16[256,256]{1,0:T(8,128)(2,1)} %w_proj.1, f32[8,2535]{1,0:T(8,128)} %rel.1, ...), custom_call_target="tpu_custom_call" | custom-call | flops 1000000000 | bytes 3000000 | tf_op jit(solution)/shard_map/pallas_call | solution.py:425
  51.1 0.0 copy-start
  51.1 1.7 %copy.12 = bf16[8,7,7,256]{3,0,2,1:T(8,128)(2,1)} copy(bf16[8,7,7,256]{3,0,2,1:T(8,128)(2,1)} %bitcast.15) | data formatting | bytes 401408
  52.7 0.0 copy-done
  52.7 0.0 copy-start.1
  52.7 0.7 %copy.13 = bf16[8,7,7,256]{3,0,2,1:T(8,128)(2,1)} copy(bf16[8,7,7,256]{3,0,2,1:T(8,128)(2,1)S(1)} %bitcast.14) | data formatting | bytes 401408
  53.4 0.0 copy-done.1
  53.5 0.6 %copy.14 = f32[256,16]{0,1:T(8,128)} copy(f32[256,16]{0,1:T(8,128)S(1)} %bitcast.16) | data formatting | bytes 32768
Async XLA Ops:
  51.1 1.7 %copy-start = (bf16[49,8,256]{2,1,0:T(8,128)(2,1)S(1)}, bf16[49,8,256]{2,1,0:T(8,128)(2,1)}, u32[]{:S(2)}) copy-start(bf16[49,8,256]{2,1,0:T(8,128)(2,1)} %get-tuple-element.7) | copy-start | bytes 602116
  52.7 0.7 %copy-start.1 = (f32[16,256]{1,0:T(8,128)S(1)}, f32[16,256]{1,0:T(8,128)}, u32[]{:S(2)}) copy-start(f32[16,256]{1,0:T(8,128)} %get-tuple-element.8) | copy-start | bytes 49156
